TPU v7x, 256 devices: a whole 4x4x8 slice. The times are simulated.
256 devices in a mesh: vp: 64 (over y_hi, z, x), ch: 4 (over y_lo, core).
Axes of the slice: x: 4, y: 4 (y_hi: 2, y_lo: 2; y = y_hi * 2 + y_lo), z: 8, core: 2. Of those that a mesh axis runs over, the one named last changes fastest.
Arguments:
- chol_a: bfloat16 [640, 4, 6000], P('vp', None, 'ch'), may hold values from -0.078125 to 0.078125
- chol_b: bfloat16 [6000, 64, 640], P('ch', 'vp'), may hold values from -6 to 6
- amplitudes: bfloat16 [640, 8, 640], P('vp'), may hold values from -0.0390625 to 0.0390625
- vir_a: float32 [4], replicated, may hold values from 0.2 to 3
- vir_b: float32 [64], P('vp'), may hold values from 0.2 to 3
- occ_pair: float32 [8], P('ch'), may hold values from -4 to -1
Outputs:
- increment: float32 [4, 64, 8], P(None, 'vp', 'ch')
All inputs are finite; a program needn't handle non-finite values.
Results may differ from a plain program's by a relative error of at most 0.0029.
Values may be sent and summed in bfloat16 or wider, within the bound.
A program may use at most 64 MiB of HBM per device.

v0:
```python
import jax
import jax.numpy as jnp
from jax import lax
from jax.sharding import PartitionSpec as P


def body(chol_a, chol_b, amplitudes, vir_a, vir_b, occ_pair):
    nch_dev = chol_b.shape[0]
    nb_dev = chol_b.shape[1]
    vir_count = chol_b.shape[2]
    a_count = chol_a.shape[1]
    pair_count = amplitudes.shape[1]
    cholesky_right = chol_b.reshape(nch_dev, nb_dev * vir_count)
    panel_rows = lax.all_gather(chol_a, "vp", axis=0, tiled=True)
    rows_here = panel_rows.shape[0]
    v_rows = jnp.dot(
        panel_rows.reshape(rows_here * a_count, nch_dev),
        cholesky_right,
        preferred_element_type=jnp.float32,
    )
    v_all = v_rows.astype(jnp.bfloat16).reshape(rows_here, a_count * nb_dev, vir_count)
    v_rows = v_all
    ladder = jnp.einsum(
        "cxd,cid->xi",
        v_rows,
        lax.all_gather(amplitudes, "vp", axis=0, tiled=True),
        preferred_element_type=jnp.float32,
    )
    ladder = ladder.reshape(a_count, nb_dev, pair_count)
    ladder = lax.psum_scatter(ladder, "ch", scatter_dimension=2, tiled=True)
    energy_gap = vir_a[:, None, None] + vir_b[None, :, None] - occ_pair[None, None, :]
    return ladder / energy_gap


def solution(mesh):
    return jax.shard_map(
        body,
        mesh=mesh,
        in_specs=(
            P("vp", None, "ch"),
            P("ch", "vp", None),
            P("vp", None, None),
            P(),
            P("vp"),
            P("ch"),
        ),
        out_specs=P(None, "vp", "ch"),
        check_vma=False,
    )
```

profile of v0, /device:TPU:1, one launch (start us, length us, event | category | flops | bytes accessed | tf_op | source)
XLA Modules:
  0.0 319.8 jit_solution(13884789636193917193)
XLA Ops:
  6.5 0.0 copy-start
  6.5 0.0 all-gather.3.cloned.1.call-start
  6.5 0.7 all-gather.3.cloned.1.call-update
  7.3 0.0 all-gather.5.cloned.1.call-start
  7.3 0.7 all-gather.5.cloned.1.call-update
  8.7 1.3 dynamic-slice
  10.6 0.7 broadcast_add_fusion
  11.2 145.8 %all-gather.3.cloned.1.call-done = bf16[640,4,1500]{2,1,0:T(4,128)(2,1)} async-done(((bf16[10,4,1500]{2,1,0:T(4,128)(2,1)}), bf16[640,4,1500]{2,1,0:T(4,128)(2,1)}) %all-gather.3.cloned.1.call-update) | async-done | bytes 7680016 | tf_op jit(solution)/shard_map/all_gather | solution.py:14
  157.0 13.2 %reshape.60 = bf16[2560,1500]{1,0:T(8,128)(2,1)} reshape(bf16[640,4,1500]{2,1,0:T(4,128)(2,1)} %all-gather.3.cloned.1.call-done) | data formatting | bytes 15360000 | tf_op jit(solution)/shard_map/reshape | solution.py:17
  170.2 0.0 copy-done
  170.2 9.7 %convolution_convert_fusion = bf16[2560,640]{1,0:T(8,128)(2,1)} fusion(bf16[2560,1500]{1,0:T(8,128)(2,1)} %reshape.60, bf16[1500,1,640]{2,0,1:T(8,128)(2,1)S(1)} %copy-done), kind=kOutput, calls=%fused_computation | convolution fusion | flops 4916838400 | bytes 12876800 | tf_op jit(solution)/shard_map/dot_general | solution.py:16
  180.0 6.5 %reshape.62 = bf16[640,4,640]{2,1,0:T(4,128)(2,1)} reshape(bf16[2560,640]{1,0:T(8,128)(2,1)} %convolution_convert_fusion) | data formatting | bytes 6553600 | tf_op jit(solution)/shard_map/reshape | solution.py:21
  186.5 0.0 copy-start.1
  186.5 108.7 %all-gather.5.cloned.1.call-done = bf16[640,8,640]{2,1,0:T(8,128)(2,1)} async-done(((bf16[10,8,640]{2,1,0:T(8,128)(2,1)}), bf16[640,8,640]{2,1,0:T(8,128)(2,1)}) %all-gather.5.cloned.1.call-update) | async-done | bytes 6553616 | tf_op jit(solution)/shard_map/all_gather | solution.py:26
  295.2 8.2 %fusion.1 = f32[4,8,1]{0,1,2:T(8,128)S(1)} fusion(bf16[640,4,640]{2,1,0:T(4,128)(2,1)} %reshape.62, bf16[640,8,640]{2,1,0:T(8,128)(2,1)} %all-gather.5.cloned.1.call-done), kind=kOutput, calls=%fused_computation.5 | convolution fusion | flops 26214400 | bytes 9830528 | tf_op jit(solution)/shard_map/cxd,cid->xi/dot_general | solution.py:23
  303.3 9.0 %all-reduce = f32[4,1,8]{0,1,2:T(1,128)S(1)} all-reduce(f32[4,1,8]{0,1,2:T(1,128)S(1)} %bitcast.14), channel_id=2, replica_groups=mesh['vp'=64,'ch'=4] {'ch'}, use_global_device_ids=true, to_apply=%region_0.0.clone | all-reduce | flops 32 | bytes 256
  312.3 0.0 copy-done.1
  312.3 0.6 subtract_divide_fusion
  (1 shorter events, 0.0 us)
Async XLA Ops:
  6.5 163.7 %copy-start = (bf16[1500,1,640]{2,0,1:T(8,128)(2,1)S(1)}, bf16[1500,1,640]{2,0,1:T(8,128)(2,1)}, u32[]{:S(2)}) copy-start(bf16[1500,1,640]{2,0,1:T(8,128)(2,1)} %param.7) | copy-start | bytes 5760004
  6.5 150.5 %all-gather.3.cloned.1.call-start = ((), (), s32[]{:S(2)}) async-start(), calls=%async_computation | async-start | bytes 7987200 | tf_op jit(solution)/shard_map/all_gather | solution.py:14
  7.3 287.9 %all-gather.5.cloned.1.call-start = ((), (), s32[]{:S(2)}) async-start(), calls=%async_computation.1 | async-start | bytes 6656000 | tf_op jit(solution)/shard_map/all_gather | solution.py:26
  186.5 125.9 %copy-start.1 = (f32[2]{0:T(128)S(1)}, f32[2]{0:T(128)}, u32[]{:S(2)}) copy-start(f32[2]{0:T(128)} %param.11) | copy-start | bytes 28
Sparse Core Ops, SparseCore 0:
  11.0 145.9 all-gather.2
  160.5 134.6 all-gather.4
where the time goes:
time: 320 us
  waiting for transfers between devices  256 us (80%)
  local copies, waits for them, and re-layouts  21 us (7%)
  matrix products  17.9 us (6%)
  between operations  14.7 us (5%)
  blocking collectives  8.96 us (3%)
    all_gather x1, waiting for transfers between devices, body(): panel_rows = lax.all_gather(chol_a, 'vp', axis=0, tiled=True)  146 us
    all_gather x1, waiting for transfers between devices, body(): lax.all_gather(amplitudes, 'vp', axis=0, tiled=True)  109 us
    reshape x1, local copies, waits for them, and re-layouts, body(): panel_rows.reshape(rows_here * a_count, nch_dev)  13.2 us
    dot_general x1, matrix products, body(): jnp.dot(panel_rows.reshape(rows_here * a_count, nch_dev), cholesky_right,...  9.73 us
    unnamed x1, blocking collectives  8.96 us
    dot_general x1, matrix products, body(): jnp.einsum('cxd,cid->xi', v_rows, lax.all_gather(amplitudes, 'vp', axis=0...  8.17 us
    reshape x1, local copies, waits for them, and re-layouts, body(): v_rows.astype(jnp.bfloat16).reshape(rows_here, a_count * nb_dev, vir_count)  6.49 us
  transfers between devices with their start and end apart: 2, of which 2 were waited for; matrix products, arithmetic and copies ran while one was open for 10% of the time, Pallas kernels for 0%

commit v1 on v0

v1 whole, which is shorter than its diff:
```python
import functools

import jax
import jax.numpy as jnp
from jax import lax
from jax.experimental import pallas as pl
from jax.experimental.pallas import tpu as pltpu
from jax.sharding import PartitionSpec as P

MESH = pl.DeviceIdType.MESH
NX, NZ = 4, 8
PQ = 384
BF16, F32 = jnp.bfloat16, jnp.float32


def kernel(a_in, b_in, t_in, out, a_stage, a_buf, t_buf, b_buf, hl, g_acc, r_send, r_in,
           a_ssem, a_rsem, t_ssem, t_rsem, b_ssem, b_rsem, f_ssem, f_rsem,
           za_ssem, za_rsem, zt_ssem, zt_rsem, y_ssem, y_rsem, r_ssem, r_rsem, l_sem):
    vp, ch = lax.axis_index("vp"), lax.axis_index("ch")
    x, z, h = vp % NX, (vp // NX) % NZ, vp // (NX * NZ)
    k, l = ch % 2, ch // 2

    def dev(x_, z_, h_, l_, k_):
        return (h_ * (NX * NZ) + z_ * NX + x_, l_ * 2 + k_)

    def remote(src, dst, ssem, rsem, device):
        return pltpu.make_async_remote_copy(
            src_ref=src, dst_ref=dst, send_sem=ssem, recv_sem=rsem, device_id=device, device_id_type=MESH)

    sibling = dev(x, z, h, l, 1 - k)
    up, down = (z + 1) % NZ, (z + NZ - 1) % NZ
    above, below = dev(x, up, h, l, k), dev(x, down, h, l, k)
    across = dev(x, z, 1 - h, 1 - l, h)
    mine = k == h

    barrier = pltpu.get_barrier_semaphore()
    q32 = x * 8 + h * 4 + l * 2 + k

    def greet(i, carry):
        q = (q32 + i) % 32
        pl.semaphore_signal(barrier, inc=1, device_id=dev(q // 8, z, (q // 4) % 2, (q // 2) % 2, q % 2),
                            device_id_type=MESH)
        return carry

    lax.fori_loop(1, 32, greet, 0)
    pl.semaphore_signal(barrier, inc=1, device_id=above, device_id_type=MESH)
    pl.semaphore_signal(barrier, inc=1, device_id=below, device_id_type=MESH)
    pl.semaphore_wait(barrier, 33)

    slot = 2 * x + k
    a_copies = []
    for dh in range(2):
        for dx in range(NX):
            to_x, to_h = (x + dx) % NX, (h + dh) % 2
            copy = remote(a_in.at[to_x], a_stage.at[slot], a_ssem.at[dh * NX + dx], a_rsem.at[slot],
                          dev(to_x, z, to_h, l, h))
            if dh == 0 and dx == 0:
                @pl.when(mine)
                def _():
                    pltpu.make_async_copy(a_in.at[x], a_stage.at[slot], a_rsem.at[slot]).start()

                @pl.when(jnp.logical_not(mine))
                def _():
                    copy.start()
            else:
                copy.start()
            a_copies.append(copy)

    t_own = pl.ds(pl.multiple_of(80 * x, 16), 80)
    t_copies = []
    for dx in range(1, NX):
        t_copies.append(remote(t_in, t_buf.at[z, t_own], t_ssem.at[dx], t_rsem.at[dx], dev((x + dx) % NX, z, h, l, k)))
    t_local = pltpu.make_async_copy(t_in, t_buf.at[z, t_own], l_sem.at[0])

    @pl.when(mine)
    def _():
        for copy in t_copies:
            copy.start()
        t_local.start()

    def b_rows(core):
        return pl.ds(pl.multiple_of(core * PQ, PQ), PQ)

    def b_quarter(q):
        return pl.ds(pl.multiple_of(q * PQ, PQ), PQ)

    b_copies = {}
    for dx in (1, 3, 2):
        to_x = (x + dx) % NX
        b_copies[dx] = remote(b_in.at[b_quarter(to_x)], b_buf.at[x, b_rows(k)], b_ssem.at[dx], b_rsem.at[dx],
                              dev(to_x, z, h, l, k))
        b_copies[dx].start()
    b_local = pltpu.make_async_copy(b_in.at[b_quarter(x)], b_buf.at[x, b_rows(k)], l_sem.at[1])
    b_local.start()
    f_copies = {0: remote(b_in.at[b_quarter(x)], b_buf.at[x, b_rows(k)], f_ssem.at[0], f_rsem.at[0], sibling)}
    f_copies[0].start()

    def ring(buf, ssem, rsem, half, step):
        lo_block, hi_block = (z + NZ - step) % NZ, (z + step) % NZ
        if step < 3:
            lo_ref, hi_ref = buf.at[lo_block], buf.at[hi_block]
        else:
            lo_ref, hi_ref = buf.at[lo_block, pl.ds(0, half)], buf.at[hi_block, pl.ds(half, half)]
        return (remote(lo_ref, lo_ref, ssem.at[2 * step], rsem.at[2 * step], above),
                remote(hi_ref, hi_ref, ssem.at[2 * step + 1], rsem.at[2 * step + 1], below))

    def arrived(buf, ssem, rsem, half, step):
        lo_block, hi_block = (z + NZ - 1 - step) % NZ, (z + 1 + step) % NZ
        if step < 3:
            lo_ref, hi_ref = buf.at[lo_block], buf.at[hi_block]
        else:
            lo_ref, hi_ref = buf.at[lo_block, pl.ds(0, half)], buf.at[hi_block, pl.ds(half, half)]
        remote(lo_ref, lo_ref, ssem.at[2 * step], rsem.at[2 * step], below).wait_recv()
        remote(hi_ref, hi_ref, ssem.at[2 * step + 1], rsem.at[2 * step + 1], above).wait_recv()

    za = functools.partial(ring, a_buf, za_ssem, za_rsem, 80)
    zt = functools.partial(ring, t_buf, zt_ssem, zt_rsem, 160)

    def y_copy(offset):
        block = (z + offset) % NZ
        return remote(t_buf.at[block], t_buf.at[block], y_ssem.at[offset], y_rsem.at[offset], across)

    for origin in range(2 * NX):
        remote(a_stage.at[origin], a_stage.at[origin], a_ssem.at[0], a_rsem.at[origin], sibling).wait_recv()
    for part in range(2):
        rows = [a_stage[2 * origin + part].astype(F32) for origin in range(NX)]
        a_buf[z, :, part * PQ:(part + 1) * PQ] = jnp.concatenate(rows, axis=0).astype(BF16)
    for copy in za(0):
        copy.start()

    @pl.when(mine)
    def _():
        for dx in range(1, NX):
            origin = pl.ds(pl.multiple_of(80 * ((x + NX - dx) % NX), 16), 80)
            remote(t_buf.at[z, origin], t_buf.at[z, origin], t_ssem.at[dx], t_rsem.at[dx], sibling).wait_recv()
        t_local.wait()
        for copy in zt(0):
            copy.start()
        y_copy(0).start()

    g_acc[...] = jnp.zeros_like(g_acc)

    def advance(step):
        arrived(a_buf, za_ssem, za_rsem, 80, step)
        if step < 3:
            for copy in za(step + 1):
                copy.start()

        @pl.when(mine)
        def _():
            arrived(t_buf, zt_ssem, zt_rsem, 160, step)
            if step < 3:
                for copy in zt(step + 1):
                    copy.start()
            for offset in ((1 + step, 7 - step) if step < 3 else (4,)):
                y_copy(offset).start()

    def t_here(*offsets):
        @pl.when(jnp.logical_not(mine))
        def _():
            for offset in offsets:
                y_copy(offset).wait_recv()

    def b_arrived(dx):
        origin = (x + NX - dx) % NX
        ref = b_buf.at[origin, b_rows(k)]
        remote(ref, ref, b_ssem.at[dx], b_rsem.at[dx], sibling).wait_recv()
        f_copies[dx] = remote(ref, ref, f_ssem.at[dx], f_rsem.at[dx], sibling)
        f_copies[dx].start()

    def compute(first, second):
        blocks = ((z + first) % NZ, (z + second) % NZ)

        def product(b, carry):
            left = jnp.concatenate([a_buf[blocks[0]], a_buf[blocks[1]]], axis=0)
            v = jnp.dot(left, b_buf[b], preferred_element_type=F32)
            high = v.astype(BF16)
            low = (v - high.astype(F32)).astype(BF16)
            for j in range(4):
                hl[j, pl.ds(pl.multiple_of(b * 160, 16), 80)] = high[80 * j:80 * j + 80]
                hl[j, pl.ds(pl.multiple_of(b * 160 + 80, 16), 80)] = low[80 * j:80 * j + 80]
            return carry

        lax.fori_loop(0, NX, product, 0)
        for j in range(4):
            g_acc[...] += lax.dot_general(
                hl[j], t_buf[blocks[j // 2], 160 * (j % 2):160 * (j % 2) + 160],
                (((1,), (1,)), ((), ())), preferred_element_type=F32)

    advance(0)
    b_arrived(1)
    b_arrived(3)
    advance(1)
    b_arrived(2)
    b_local.wait()
    for dx in range(NX):
        ref = b_buf.at[(x + NX - dx) % NX, b_rows(1 - k)]
        remote(ref, ref, f_ssem.at[dx], f_rsem.at[dx], sibling).wait_recv()
    t_here(0, 1)
    compute(0, 1)
    advance(2)
    t_here(7, 2)
    compute(7, 2)
    t_here(6, 3)
    compute(6, 3)
    advance(3)
    t_here(5, 4)
    compute(5, 4)

    row = lax.broadcasted_iota(jnp.int32, (80, 160), 0)
    col = lax.broadcasted_iota(jnp.int32, (80, 160), 1)
    diagonal = (row // 4) == (col // 8)
    left = ((lax.broadcasted_iota(jnp.int32, (8, 80), 1) % 4) == lax.broadcasted_iota(jnp.int32, (8, 80), 0)).astype(F32)
    right = ((lax.broadcasted_iota(jnp.int32, (160, 128), 0) % 8)
             == lax.broadcasted_iota(jnp.int32, (160, 128), 1)).astype(F32)
    for b in range(NX):
        both = g_acc[160 * b:160 * b + 80] + g_acc[160 * b + 80:160 * b + 160]
        both = jnp.where(diagonal, both, 0.0)
        half = jnp.dot(left, both, precision=lax.Precision.HIGHEST, preferred_element_type=F32)
        r_send[b] = jnp.dot(half, right, precision=lax.Precision.HIGHEST, preferred_element_type=F32)

    q16 = x * 4 + l * 2 + k
    r_copies = []
    for d in range(1, 16):
        q = (q16 + d) % 16
        copy = remote(r_send.at[q // 4], r_in.at[d], r_ssem.at[d], r_rsem.at[d],
                      dev(q // 4, z, h, (q // 2) % 2, q % 2))
        copy.start()
        r_copies.append(copy)
    total = r_send[x]
    for d, copy in enumerate(r_copies, 1):
        copy.wait_recv()
        total = total + r_in[d]
    out[...] = total

    for copy in r_copies:
        copy.wait_send()
    for i, copy in enumerate(a_copies):
        if i == 0:
            @pl.when(jnp.logical_not(mine))
            def _():
                copy.wait_send()
        else:
            copy.wait_send()
    for dx in (1, 2, 3):
        b_copies[dx].wait_send()
    for dx in range(NX):
        f_copies[dx].wait_send()
    for step in range(4):
        for copy in za(step):
            copy.wait_send()

    @pl.when(mine)
    def _():
        for copy in t_copies:
            copy.wait_send()
        for step in range(4):
            for copy in zt(step):
                copy.wait_send()
        for offset in range(NZ):
            y_copy(offset).wait_send()


def body(chol_a, chol_b, amplitudes, vir_a, vir_b, occ_pair):
    a_in = jnp.pad(chol_a.reshape(40, 1500), ((0, 0), (0, NX * PQ - 1500)))
    a_in = a_in.reshape(40, NX, PQ).transpose(1, 0, 2)
    b_in = jnp.pad(chol_b.reshape(1500, 640), ((0, NX * PQ - 1500), (0, 0)))
    t_in = amplitudes.reshape(80, 640)
    dma = pltpu.SemaphoreType.DMA
    tile = pl.pallas_call(
        kernel,
        out_shape=jax.ShapeDtypeStruct((8, 128), F32),
        in_specs=[pl.BlockSpec(memory_space=pltpu.VMEM), pl.BlockSpec(memory_space=pl.ANY),
                  pl.BlockSpec(memory_space=pltpu.VMEM)],
        out_specs=pl.BlockSpec(memory_space=pltpu.VMEM),
        scratch_shapes=[
            pltpu.VMEM((2 * NX, 40, PQ), BF16),
            pltpu.VMEM((NZ, 160, 2 * PQ), BF16),
            pltpu.VMEM((NZ, 320, 640), BF16),
            pltpu.VMEM((NX, 2 * PQ, 640), BF16),
            pltpu.VMEM((4, 640, 640), BF16),
            pltpu.VMEM((640, 160), F32),
            pltpu.VMEM((NX, 8, 128), F32),
            pltpu.VMEM((16, 8, 128), F32),
            dma((8,)), dma((8,)), dma((4,)), dma((4,)), dma((4,)), dma((4,)), dma((4,)), dma((4,)),
            dma((8,)), dma((8,)), dma((8,)), dma((8,)), dma((8,)), dma((8,)), dma((16,)), dma((16,)), dma((2,)),
        ],
        compiler_params=pltpu.CompilerParams(
            collective_id=0, has_side_effects=True, vmem_limit_bytes=48 * 1024 * 1024),
        cost_estimate=pl.CostEstimate(flops=7_000_000_000, bytes_accessed=16_000_000, transcendentals=0),
    )(a_in, b_in, t_in)
    pairs = occ_pair.shape[0]
    ladder = lax.dynamic_slice_in_dim(tile[:4], lax.axis_index("ch") * pairs, pairs, 1)
    energy_gap = vir_a[:, None, None] + vir_b[None, :, None] - occ_pair[None, None, :]
    return ladder[:, None, :] / energy_gap


def solution(mesh):
    return jax.shard_map(
        body,
        mesh=mesh,
        in_specs=(
            P("vp", None, "ch"),
            P("ch", "vp", None),
            P("vp", None, None),
            P(),
            P("vp"),
            P("ch"),
        ),
        out_specs=P(None, "vp", "ch"),
        check_vma=False,
    )
```

time: 320 us -> 78.7 us (0.25)
  waiting for transfers between devices: 256 us -> 0 us
  Pallas kernels: 0 us -> 73.2 us
  matrix products: 17.9 us -> 0 us
  local copies, waits for them, and re-layouts: 21 us -> 3.38 us
  between operations: 14.7 us -> 0.74 us
  blocking collectives: 8.96 us -> 0 us
    all_gather x2 -> x0, waiting for transfers between devices: 254 us -> none  [the longest x1 146 us: body(): panel_rows = lax.all_gather(chol_a, 'vp', axis=0, tiled=True)]
    pallas_call x0 -> x1, Pallas kernels: none -> 73.2 us  [body(): pl.pallas_call(kernel, out_shape=jax.ShapeDtypeStruct((8, 128), F32), in_...]
    reshape x2, local copies, waits for them, and re-layouts: 19.7 us -> 0.95 us  [the longest x1 0.94 us: body(): a_in = jnp.pad(chol_a.reshape(40, 1500), ((0, 0), (0, NX * PQ - 1500)))]
    dot_general x2 -> x0, matrix products: 17.9 us -> none  [the longest x1 9.73 us: body(): jnp.dot(panel_rows.reshape(rows_here * a_count, nch_dev), cholesky_right,...]
    unnamed x1 -> x0, blocking collectives: 8.96 us -> none
  transfers between devices with their start and end apart: 2 -> 0, of which waited for: 2 -> 0; matrix products, arithmetic and copies ran while one was open for 10% -> 0% of each run, Pallas kernels for 0% -> 0%
where the time goes in v1:
time: 78.7 us; the launch traced here: 77.4 us
  Pallas kernels  73.2 us (93%)
  local copies, waits for them, and re-layouts  3.38 us (4%)
    pallas_call x1, Pallas kernels, body(): pl.pallas_call(kernel, out_shape=jax.ShapeDtypeStruct((8, 128), F32), in_...  73.2 us
    pad x1, local copies, waits for them, and re-layouts, body(): b_in = jnp.pad(chol_b.reshape(1500, 640), ((0, NX * PQ - 1500), (0, 0)))  1.74 us

profile of v1, /device:TPU:1, one launch (start us, length us, event | category | flops | bytes accessed | tf_op | source)
XLA Modules:
  0.0 77.4 jit_solution(11789160337955326585)
XLA Ops:
  0.0 0.9 %reshape.24 = bf16[40,1500]{1,0:T(8,128)(2,1)S(1)} reshape(bf16[10,4,1500]{2,1,0:T(4,128)(2,1)} %param.6) | data formatting | bytes 240000 | tf_op jit(solution)/shard_map/reshape | solution.py:265
  1.0 0.0 copy-start
  1.0 1.7 %pad.9.b_in = bf16[1536,640]{1,0:T(8,128)(2,1)S(1)} pad(bf16[1500,640]{1,0:T(8,128)(2,1)} %bitcast.14, bf16[]{:T(256)} %constant.2.clone.1), padding=0_36x0_0 | pad | bytes 3886082 | tf_op jit(solution)/shard_map/jit(_pad)/pad | solution.py:267
  2.7 0.0 copy-done
  2.7 0.0 copy-start.2
  2.8 0.0 copy-start.1
  2.8 73.2 %shard_map.64 = f32[8,128]{1,0:T(8,128)S(1)} custom-call(bf16[4,40,384]{2,1,0:T(8,128)(2,1)S(1)} %bitcast.12, bf16[1536,640]{1,0:T(8,128)(2,1)S(1)} %pad.9.b_in, bf16[80,640]{1,0:T(8,128)(2,1)S(1)} %bitcast.13), custom_call_target="tpu_custom_call" | custom-call | flops 7000000000 | bytes 16000000 | tf_op jit(solution)/shard_map/pallas_call | solution.py:270
  76.7 0.0 copy-done.2
  76.7 0.0 copy-done.1
  76.7 0.1 subtract_divide_fusion
  76.8 0.7 copy.9
  (4 shorter events, 0.0 us)
Async XLA Ops:
  1.0 1.8 %copy-start = (bf16[10,8,640]{2,1,0:T(8,128)(2,1)S(1)}, bf16[10,8,640]{2,1,0:T(8,128)(2,1)}, u32[]{:S(2)}) copy-start(bf16[10,8,640]{2,1,0:T(8,128)(2,1)} %param.8) | copy-start | bytes 307204
  2.7 73.9 %copy-start.2 = (f32[4]{0:T(128)S(1)}, f32[4]{0:T(128)}, u32[]{:S(2)}) copy-start(f32[4]{0:T(128)} %param.9) | copy-start | bytes 52
  2.8 73.9 %copy-start.1 = (f32[2]{0:T(128)S(1)}, f32[2]{0:T(128)}, u32[]{:S(2)}) copy-start(f32[2]{0:T(128)} %param.11) | copy-start | bytes 28

commit v2 on v1

v2 whole, which is shorter than its diff:
```python
import functools

import jax
import jax.numpy as jnp
from jax import lax
from jax.experimental import pallas as pl
from jax.experimental.pallas import tpu as pltpu
from jax.sharding import PartitionSpec as P

MESH = pl.DeviceIdType.MESH
NX, NZ = 4, 8
PQ = 384
SLOTS = (0, 1, 3, 2)
BF16, F32 = jnp.bfloat16, jnp.float32


def kernel(a_in, b_in, t_in, out, a_stage, a_buf, t_buf, b_buf, hl, g_acc, r_send, r_in,
           a_ssem, a_rsem, t_ssem, t_rsem, b_ssem, b_rsem, f_ssem, f_rsem,
           za_ssem, za_rsem, zt_ssem, zt_rsem, p_ssem, p_rsem, c_ssem, c_rsem, d_ssem, d_rsem,
           r_ssem, r_rsem, l_sem):
    vp, ch = lax.axis_index("vp"), lax.axis_index("ch")
    x, z, h = vp % NX, (vp // NX) % NZ, vp // (NX * NZ)
    k, l = ch % 2, ch // 2

    def dev(x_, z_, h_, l_, k_):
        return (h_ * (NX * NZ) + z_ * NX + x_, l_ * 2 + k_)

    def remote(src, dst, ssem, rsem, device):
        return pltpu.make_async_remote_copy(
            src_ref=src, dst_ref=dst, send_sem=ssem, recv_sem=rsem, device_id=device, device_id_type=MESH)

    def rows(start, size):
        return pl.ds(pl.multiple_of(start, 16), size)

    sibling = dev(x, z, h, l, 1 - k)
    above, below = dev(x, (z + 1) % NZ, h, l, k), dev(x, (z + NZ - 1) % NZ, h, l, k)
    pair = dev(x, z, h, 1 - l, k)
    across = dev(x, z, 1 - h, 1 - l, k)
    mine = k == h
    other = jnp.logical_not(mine)

    barrier = pltpu.get_barrier_semaphore()
    q32 = x * 8 + h * 4 + l * 2 + k

    def greet(i, carry):
        q = (q32 + i) % 32
        pl.semaphore_signal(barrier, inc=1, device_id=dev(q // 8, z, (q // 4) % 2, (q // 2) % 2, q % 2),
                            device_id_type=MESH)
        return carry

    lax.fori_loop(1, 32, greet, 0)
    pl.semaphore_signal(barrier, inc=1, device_id=above, device_id_type=MESH)
    pl.semaphore_signal(barrier, inc=1, device_id=below, device_id_type=MESH)
    pl.semaphore_wait(barrier, 33)

    slot = 2 * x + k
    a_copies = []
    for dh in range(2):
        for dx in range(NX):
            to_x, to_h = (x + dx) % NX, (h + dh) % 2
            copy = remote(a_in.at[to_x], a_stage.at[slot], a_ssem.at[dh * NX + dx], a_rsem.at[slot],
                          dev(to_x, z, to_h, l, h))
            if dh == 0 and dx == 0:
                @pl.when(mine)
                def _():
                    pltpu.make_async_copy(a_in.at[x], a_stage.at[slot], a_rsem.at[slot]).start()

                @pl.when(other)
                def _():
                    copy.start()
            else:
                copy.start()
            a_copies.append(copy)

    t_copies = [remote(t_in, t_buf.at[z, rows(80 * x, 80)], t_ssem.at[dx], t_rsem.at[x % 2],
                       dev((x + dx) % NX, z, h, l, k)) for dx in range(1, NX)]
    t_local = pltpu.make_async_copy(t_in, t_buf.at[z, rows(80 * x, 80)], t_rsem.at[x % 2])
    t_mine = jnp.logical_and(mine, x // 2 == l)

    @pl.when(t_mine)
    def _():
        for copy in t_copies:
            copy.start()
        t_local.start()

    def b_rows(core):
        return rows(core * PQ, PQ)

    def b_copy(s):
        to_x = (x + SLOTS[s]) % NX
        return remote(b_in.at[rows(to_x * PQ, PQ)], b_buf.at[s, b_rows(k)], b_ssem.at[s], b_rsem.at[s],
                      dev(to_x, z, h, l, k))

    def f_copy(s):
        src = b_in.at[rows(x * PQ, PQ)] if s == 0 else b_buf.at[s, b_rows(k)]
        return remote(src, b_buf.at[s, b_rows(k)], f_ssem.at[s], f_rsem.at[s], sibling)

    for s in range(1, NX):
        b_copy(s).start()
    b_local = pltpu.make_async_copy(b_in.at[rows(x * PQ, PQ)], b_buf.at[0, b_rows(k)], l_sem.at[0])
    b_local.start()
    f_copy(0).start()

    def last(way, half):
        return 3 if way == half else 2

    def block_of(offset):
        return (z + offset) % NZ

    def za(way, half, step, offset):
        ref = a_buf.at[block_of(offset), pl.ds(80 * half, 80)]
        i = (way * 2 + half) * 4 + step
        return remote(ref, ref, za_ssem.at[i], za_rsem.at[i], above if way == 0 else below)

    def zt(way, half, step, offset):
        ref = t_buf.at[block_of(offset), rows(160 * l + 80 * half, 80)]
        i = (way * 2 + half) * 4 + step
        return remote(ref, ref, zt_ssem.at[i], zt_rsem.at[i], above if way == 0 else below)

    def sent_offset(way, step):
        return (NZ - step) % NZ if way == 0 else step

    def got_offset(way, step):
        return NZ - 1 - step if way == 0 else 1 + step

    def unit(offset, which):
        return t_buf.at[block_of(offset), rows(160 * which, 160)]

    def quarter(offset, which, part):
        return t_buf.at[block_of(offset), rows(160 * which + 80 * part, 80)]

    def to_pair(offset, which):
        return remote(unit(offset, which), unit(offset, which), p_ssem.at[offset], p_rsem.at[offset], pair)

    def to_across(offset, which):
        return remote(unit(offset, which), unit(offset, which), c_ssem.at[offset], c_rsem.at[offset], across)

    def more_across(offset, which):
        ref = quarter(offset, which, 1)
        return remote(ref, ref, d_ssem.at[offset], d_rsem.at[offset], across)

    def more_pair(offset, which):
        ref = quarter(offset, which, 0)
        return remote(ref, ref, p_ssem.at[offset], p_rsem.at[offset], pair)

    for origin in range(2 * NX):
        remote(a_stage.at[origin], a_stage.at[origin], a_ssem.at[0], a_rsem.at[origin], sibling).wait_recv()
    for part in range(2):
        pieces = [a_stage[2 * origin + part].astype(F32) for origin in range(NX)]
        a_buf[z, :, part * PQ:(part + 1) * PQ] = jnp.concatenate(pieces, axis=0).astype(BF16)
    for half in range(2):
        for way in range(2):
            za(way, half, 0, 0).start()

    @pl.when(mine)
    def _():
        for half in range(2):
            ref = quarter(0, l, half)
            remote(ref, ref, t_ssem.at[0], t_rsem.at[half], sibling).wait_recv()
            for way in range(2):
                zt(way, half, 0, 0).start()
        to_pair(0, l).start()
        to_across(0, l).start()

    g_acc[...] = jnp.zeros_like(g_acc)

    def arrive(step):
        for half in range(2):
            ways = [way for way in range(2) if step <= last(way, half)]
            for way in ways:
                offset = got_offset(way, step)
                za(way, half, step, offset).wait_recv()
                if step < last(way, half):
                    za(way, half, step + 1, offset).start()

            @pl.when(mine)
            def _():
                for way in ways:
                    offset = got_offset(way, step)
                    zt(way, half, step, offset).wait_recv()
                    if step < last(way, half):
                        zt(way, half, step + 1, offset).start()

        @pl.when(mine)
        def _():
            for offset in ((7 - step, 1 + step) if step < 3 else (4,)):
                to_pair(offset, l).start()
                to_across(offset, l).start()

    def relay(*offsets):
        @pl.when(mine)
        def _():
            for offset in offsets:
                to_pair(offset, 1 - l).wait_recv()
                more_across(offset, 1 - l).start()

        @pl.when(other)
        def _():
            for offset in offsets:
                to_across(offset, 1 - l).wait_recv()
                more_pair(offset, 1 - l).start()

    def complete(*offsets):
        @pl.when(other)
        def _():
            for offset in offsets:
                more_across(offset, l).wait_recv()
                more_pair(offset, l).wait_recv()

    def b_arrived(s):
        ref = b_buf.at[s, b_rows(k)]
        remote(ref, ref, b_ssem.at[s], b_rsem.at[s], sibling).wait_recv()
        f_copy(s).start()

    def b_complete(s):
        if s == 0:
            b_local.wait()
        ref = b_buf.at[s, b_rows(1 - k)]
        remote(ref, ref, f_ssem.at[s], f_rsem.at[s], sibling).wait_recv()

    groups = ((0, 1), (7, 2), (6, 3), (5, 4))

    def product(g, first, end):
        blocks = [block_of(offset) for offset in groups[g]]

        def one(b, carry):
            left = jnp.concatenate([a_buf[blocks[0]], a_buf[blocks[1]]], axis=0)
            v = jnp.dot(left, b_buf[b], preferred_element_type=F32)
            high = v.astype(BF16)
            low = (v - high.astype(F32)).astype(BF16)
            for j in range(4):
                hl[4 * g + j, rows(b * 160, 80)] = high[80 * j:80 * j + 80]
                hl[4 * g + j, rows(b * 160 + 80, 80)] = low[80 * j:80 * j + 80]
            return carry

        lax.fori_loop(first, end, one, 0)

    def contract(g):
        for j in range(4):
            g_acc[...] += lax.dot_general(
                hl[4 * g + j], t_buf[block_of(groups[g][j // 2]), 160 * (j % 2):160 * (j % 2) + 160],
                (((1,), (1,)), ((), ())), preferred_element_type=F32)

    arrive(0)
    relay(0)
    b_complete(0)
    product(0, 0, 1)
    b_arrived(1)
    b_arrived(2)
    arrive(1)
    relay(7, 1)
    b_complete(1)
    b_complete(2)
    product(0, 1, 3)
    product(1, 0, 3)
    b_arrived(3)
    b_complete(3)
    product(0, 3, 4)
    product(1, 3, 4)
    arrive(2)
    relay(6, 2)
    complete(0, 1)
    contract(0)
    product(2, 0, 4)
    complete(7, 2)
    contract(1)
    arrive(3)
    relay(5, 3)
    product(3, 0, 4)
    relay(4)
    complete(6, 3)
    contract(2)
    complete(5, 4)
    contract(3)

    row = lax.broadcasted_iota(jnp.int32, (80, 160), 0)
    col = lax.broadcasted_iota(jnp.int32, (80, 160), 1)
    diagonal = (row // 4) == (col // 8)
    left = ((lax.broadcasted_iota(jnp.int32, (8, 80), 1) % 4) == lax.broadcasted_iota(jnp.int32, (8, 80), 0)).astype(F32)
    right = ((lax.broadcasted_iota(jnp.int32, (160, 128), 0) % 8)
             == lax.broadcasted_iota(jnp.int32, (160, 128), 1)).astype(F32)
    for s in range(NX):
        both = g_acc[160 * s:160 * s + 80] + g_acc[160 * s + 80:160 * s + 160]
        both = jnp.where(diagonal, both, 0.0)
        half = jnp.dot(left, both, precision=lax.Precision.HIGHEST, preferred_element_type=F32)
        r_send[s] = jnp.dot(half, right, precision=lax.Precision.HIGHEST, preferred_element_type=F32)

    q4 = l * 2 + k
    r_copies = []
    for s in (3, 1, 2, 0):
        for e in (2, 3, 1, 0):
            if s == 0 and e == 0:
                continue
            q = (q4 + e) % 4
            copy = remote(r_send.at[s], r_in.at[4 * s + e], r_ssem.at[4 * s + e], r_rsem.at[4 * s + e],
                          dev((x + NX - SLOTS[s]) % NX, z, h, q // 2, q % 2))
            copy.start()
            r_copies.append(copy)
    total = r_send[0]
    for copy in r_copies:
        copy.wait_recv()
    for i in range(1, 16):
        total = total + r_in[i]
    out[...] = total

    for copy in r_copies:
        copy.wait_send()
    for i, copy in enumerate(a_copies):
        if i == 0:
            @pl.when(other)
            def _():
                copy.wait_send()
        else:
            copy.wait_send()
    for s in range(NX):
        f_copy(s).wait_send()
        if s:
            b_copy(s).wait_send()
    for way in range(2):
        for half in range(2):
            for step in range(last(way, half) + 1):
                za(way, half, step, sent_offset(way, step)).wait_send()

    @pl.when(t_mine)
    def _():
        for copy in t_copies:
            copy.wait_send()

    @pl.when(mine)
    def _():
        for way in range(2):
            for half in range(2):
                for step in range(last(way, half) + 1):
                    zt(way, half, step, sent_offset(way, step)).wait_send()
        for offset in range(NZ):
            to_pair(offset, l).wait_send()
            to_across(offset, l).wait_send()
            more_across(offset, 1 - l).wait_send()

    @pl.when(other)
    def _():
        for offset in range(NZ):
            more_pair(offset, 1 - l).wait_send()


def body(chol_a, chol_b, amplitudes, vir_a, vir_b, occ_pair):
    a_in = jnp.pad(chol_a.reshape(40, 1500), ((0, 0), (0, NX * PQ - 1500)))
    a_in = a_in.reshape(40, NX, PQ).transpose(1, 0, 2)
    b_in = jnp.pad(chol_b.reshape(1500, 640), ((0, NX * PQ - 1500), (0, 0)))
    t_in = amplitudes.reshape(80, 640)
    dma = pltpu.SemaphoreType.DMA
    tile = pl.pallas_call(
        kernel,
        out_shape=jax.ShapeDtypeStruct((8, 128), F32),
        in_specs=[pl.BlockSpec(memory_space=pltpu.VMEM), pl.BlockSpec(memory_space=pl.ANY),
                  pl.BlockSpec(memory_space=pltpu.VMEM)],
        out_specs=pl.BlockSpec(memory_space=pltpu.VMEM),
        scratch_shapes=[
            pltpu.VMEM((2 * NX, 40, PQ), BF16),
            pltpu.VMEM((NZ, 160, 2 * PQ), BF16),
            pltpu.VMEM((NZ, 320, 640), BF16),
            pltpu.VMEM((NX, 2 * PQ, 640), BF16),
            pltpu.VMEM((16, 640, 640), BF16),
            pltpu.VMEM((640, 160), F32),
            pltpu.VMEM((NX, 8, 128), F32),
            pltpu.VMEM((16, 8, 128), F32),
            dma((8,)), dma((8,)), dma((4,)), dma((4,)), dma((4,)), dma((4,)), dma((4,)), dma((4,)),
            dma((16,)), dma((16,)), dma((16,)), dma((16,)), dma((8,)), dma((8,)), dma((8,)), dma((8,)), dma((8,)), dma((8,)),
            dma((16,)), dma((16,)), dma((1,)),
        ],
        compiler_params=pltpu.CompilerParams(
            collective_id=0, has_side_effects=True, vmem_limit_bytes=48 * 1024 * 1024),
        cost_estimate=pl.CostEstimate(flops=7_000_000_000, bytes_accessed=16_000_000, transcendentals=0),
    )(a_in, b_in, t_in)
    pairs = occ_pair.shape[0]
    ladder = lax.dynamic_slice_in_dim(tile[:4], lax.axis_index("ch") * pairs, pairs, 1)
    energy_gap = vir_a[:, None, None] + vir_b[None, :, None] - occ_pair[None, None, :]
    return ladder[:, None, :] / energy_gap


def solution(mesh):
    return jax.shard_map(
        body,
        mesh=mesh,
        in_specs=(
            P("vp", None, "ch"),
            P("ch", "vp", None),
            P("vp", None, None),
            P(),
            P("vp"),
            P("ch"),
        ),
        out_specs=P(None, "vp", "ch"),
        check_vma=False,
    )
```

time: 78.7 us -> 71 us (0.902)
  the two profiles are of different devices: /device:TPU:1 before, /device:TPU:25 now
where the time goes in v2:
time: 71 us; the launch traced here: 70.9 us
  Pallas kernels  66.7 us (94%)
  local copies, waits for them, and re-layouts  3.38 us (5%)
  between operations  0.74 us (1%)
    pallas_call x1, Pallas kernels, body(): pl.pallas_call(kernel, out_shape=jax.ShapeDtypeStruct((8, 128), F32), in_...  66.7 us
    pad x1, local copies, waits for them, and re-layouts, body(): b_in = jnp.pad(chol_b.reshape(1500, 640), ((0, NX * PQ - 1500), (0, 0)))  1.74 us

profile of v2, /device:TPU:25, one launch (start us, length us, event | category | flops | bytes accessed | tf_op | source)
XLA Modules:
  0.0 70.9 jit_solution(13475184722141987211)
XLA Ops:
  0.0 0.9 %reshape.24 = bf16[40,1500]{1,0:T(8,128)(2,1)S(1)} reshape(bf16[10,4,1500]{2,1,0:T(4,128)(2,1)} %param.6) | data formatting | bytes 240000 | tf_op jit(solution)/shard_map/reshape | solution.py:347
  1.0 0.0 copy-start
  1.0 1.7 %pad.9.b_in = bf16[1536,640]{1,0:T(8,128)(2,1)S(1)} pad(bf16[1500,640]{1,0:T(8,128)(2,1)} %bitcast.14, bf16[]{:T(256)} %constant.2.clone.1), padding=0_36x0_0 | pad | bytes 3886082 | tf_op jit(solution)/shard_map/jit(_pad)/pad | solution.py:349
  2.7 0.0 copy-done
  2.7 0.0 copy-start.2
  2.8 0.0 copy-start.1
  2.8 66.7 %shard_map.64 = f32[8,128]{1,0:T(8,128)S(1)} custom-call(bf16[4,40,384]{2,1,0:T(8,128)(2,1)S(1)} %bitcast.12, bf16[1536,640]{1,0:T(8,128)(2,1)S(1)} %pad.9.b_in, bf16[80,640]{1,0:T(8,128)(2,1)S(1)} %bitcast.13), custom_call_target="tpu_custom_call" | custom-call | flops 7000000000 | bytes 16000000 | tf_op jit(solution)/shard_map/pallas_call | solution.py:352
  70.1 0.0 copy-done.2
  70.2 0.0 copy-done.1
  70.2 0.1 subtract_divide_fusion
  70.3 0.7 copy.9
  (4 shorter events, 0.0 us)
Async XLA Ops:
  1.0 1.8 %copy-start = (bf16[10,8,640]{2,1,0:T(8,128)(2,1)S(1)}, bf16[10,8,640]{2,1,0:T(8,128)(2,1)}, u32[]{:S(2)}) copy-start(bf16[10,8,640]{2,1,0:T(8,128)(2,1)} %param.8) | copy-start | bytes 307204
  2.7 67.4 %copy-start.2 = (f32[4]{0:T(128)S(1)}, f32[4]{0:T(128)}, u32[]{:S(2)}) copy-start(f32[4]{0:T(128)} %param.9) | copy-start | bytes 52
  2.8 67.4 %copy-start.1 = (f32[2]{0:T(128)S(1)}, f32[2]{0:T(128)}, u32[]{:S(2)}) copy-start(f32[2]{0:T(128)} %param.11) | copy-start | bytes 28

commit v3 on v2

v3 whole, which is shorter than its diff:
```python
import functools

import jax
import jax.numpy as jnp
from jax import lax
from jax.experimental import pallas as pl
from jax.experimental.pallas import tpu as pltpu
from jax.sharding import PartitionSpec as P

MESH = pl.DeviceIdType.MESH
NX, NZ = 4, 8
PQ = 384
WINDOW = 2
SLOTS = (0, 1, 3, 2)
BF16, F32 = jnp.bfloat16, jnp.float32


def kernel(a_hbm, b_hbm, t_hbm, va_hbm, vb_hbm, occ_hbm, out, va, vb, occ, a_raw, b_in, t_in, a_in, b_end, a_stage, a_buf, t_buf, b_buf, hl, g_acc, r_send, r_in,
           a_ssem, a_rsem, t_ssem, t_rsem, b_ssem, b_rsem, f_ssem, f_rsem,
           za_ssem, za_rsem, zt_ssem, zt_rsem, p_ssem, p_rsem, c_ssem, c_rsem, d_ssem, d_rsem,
           r_ssem, r_rsem, l_sem):
    vp, ch = lax.axis_index("vp"), lax.axis_index("ch")
    x, z, h = vp % NX, (vp // NX) % NZ, vp // (NX * NZ)
    k, l = ch % 2, ch // 2

    def dev(x_, z_, h_, l_, k_):
        return (h_ * (NX * NZ) + z_ * NX + x_, l_ * 2 + k_)

    def remote(src, dst, ssem, rsem, device):
        return pltpu.make_async_remote_copy(
            src_ref=src, dst_ref=dst, send_sem=ssem, recv_sem=rsem, device_id=device, device_id_type=MESH)

    def rows(start, size):
        return pl.ds(pl.multiple_of(start, 16), size)

    sibling = dev(x, z, h, l, 1 - k)
    above, below = dev(x, (z + 1) % NZ, h, l, k), dev(x, (z + NZ - 1) % NZ, h, l, k)
    pair = dev(x, z, h, 1 - l, k)
    across = dev(x, z, 1 - h, 1 - l, k)
    mine = k == h
    other = jnp.logical_not(mine)

    loads = [pltpu.make_async_copy(src, dst, l_sem.at[1 + i])
             for i, (src, dst) in enumerate(((a_hbm, a_raw), (t_hbm, t_in), (b_hbm, b_in)))]
    energies = [pltpu.make_async_copy(src, dst, l_sem.at[4 + i])
                for i, (src, dst) in enumerate(((va_hbm, va), (vb_hbm, vb), (occ_hbm, occ)))]
    for load in loads + energies:
        load.start()

    barrier = pltpu.get_barrier_semaphore()
    q32 = x * 8 + h * 4 + l * 2 + k

    def greet(i, carry):
        q = (q32 + i) % 32
        pl.semaphore_signal(barrier, inc=1, device_id=dev(q // 8, z, (q // 4) % 2, (q // 2) % 2, q % 2),
                            device_id_type=MESH)
        return carry

    lax.fori_loop(1, 32, greet, 0)
    pl.semaphore_signal(barrier, inc=1, device_id=above, device_id_type=MESH)
    pl.semaphore_signal(barrier, inc=1, device_id=below, device_id_type=MESH)

    for load in loads:
        load.wait()
    size = a_raw.shape[2]
    for q in range(NX):
        width = min(PQ, size - q * PQ)
        piece = a_raw[:, :, q * PQ:q * PQ + width].astype(F32)
        if width < PQ:
            piece = jnp.concatenate([piece, jnp.zeros(piece.shape[:2] + (PQ - width,), F32)], axis=2)
        a_in[q] = piece.reshape(40, PQ).astype(BF16)
    start, whole = (NX - 1) * PQ, size // 16 * 16
    b_end[0:whole - start] = b_in[start:whole]
    rest = b_in[whole:size].astype(F32)
    b_end[whole - start:PQ] = jnp.concatenate(
        [rest, jnp.zeros((NX * PQ - size, rest.shape[1]), F32)], axis=0).astype(BF16)

    pl.semaphore_wait(barrier, 33)

    t_copies = [remote(t_in, t_buf.at[z, rows(80 * x, 80)], t_ssem.at[dx], t_rsem.at[x % 2],
                       dev((x + dx) % NX, z, h, l, k)) for dx in range(1, NX)]
    t_local = pltpu.make_async_copy(t_in, t_buf.at[z, rows(80 * x, 80)], t_rsem.at[x % 2])
    t_mine = jnp.logical_and(mine, x // 2 == l)

    @pl.when(t_mine)
    def _():
        for copy in t_copies:
            copy.start()
        t_local.start()

    slot = 2 * x + k
    a_copies = []
    for dh in range(2):
        for dx in range(NX):
            to_x, to_h = (x + dx) % NX, (h + dh) % 2
            copy = remote(a_in.at[to_x], a_stage.at[slot], a_ssem.at[dh * NX + dx], a_rsem.at[slot],
                          dev(to_x, z, to_h, l, h))
            if dh == 0 and dx == 0:
                @pl.when(mine)
                def _():
                    pltpu.make_async_copy(a_in.at[x], a_stage.at[slot], a_rsem.at[slot]).start()

                @pl.when(other)
                def _():
                    copy.start()
            else:
                copy.start()
            a_copies.append(copy)

    def b_rows(core):
        return rows(core * PQ, PQ)

    def b_source(q, do):
        @pl.when(q == NX - 1)
        def _():
            do(b_end)

        @pl.when(q != NX - 1)
        def _():
            do(b_in.at[rows(jnp.minimum(q, NX - 2) * PQ, PQ)])

    def b_copy(s, src):
        return remote(src, b_buf.at[s, b_rows(k)], b_ssem.at[s], b_rsem.at[s], dev((x + SLOTS[s]) % NX, z, h, l, k))

    def f_copy(s, src=None):
        src = b_buf.at[s, b_rows(k)] if src is None else src
        return remote(src, b_buf.at[s, b_rows(k)], f_ssem.at[s], f_rsem.at[s], sibling)

    def b_stay(src):
        return pltpu.make_async_copy(src, b_buf.at[0, b_rows(k)], l_sem.at[0])

    def keep(src):
        b_stay(src).start()
        f_copy(0, src).start()

    def start_b(s):
        b_source((x + SLOTS[s]) % NX, lambda src: b_copy(s, src).start())

    start_b(1)
    start_b(2)
    b_source(x, keep)

    def last(way, half):
        return 3 if way == half else 2

    def block_of(offset):
        return (z + offset) % NZ

    def za(way, half, step, offset):
        ref = a_buf.at[block_of(offset), pl.ds(80 * half, 80)]
        i = (way * 2 + half) * 4 + step
        return remote(ref, ref, za_ssem.at[i], za_rsem.at[i], above if way == 0 else below)

    def zt(way, half, step, offset):
        ref = t_buf.at[block_of(offset), rows(160 * l + 80 * half, 80)]
        i = (way * 2 + half) * 4 + step
        return remote(ref, ref, zt_ssem.at[i], zt_rsem.at[i], above if way == 0 else below)

    def sent_offset(way, step):
        return (NZ - step) % NZ if way == 0 else step

    def got_offset(way, step):
        return NZ - 1 - step if way == 0 else 1 + step

    def quarter(offset, which, part):
        return t_buf.at[block_of(offset), rows(160 * which + 80 * part, 80)]

    def to_pair(offset, which, part):
        ref = quarter(offset, which, part)
        return remote(ref, ref, p_ssem.at[2 * offset + part], p_rsem.at[2 * offset + part], pair)

    def to_across(offset, which, part):
        ref = quarter(offset, which, part)
        return remote(ref, ref, c_ssem.at[2 * offset + part], c_rsem.at[2 * offset + part], across)

    def more_across(offset, which):
        ref = quarter(offset, which, 1)
        return remote(ref, ref, d_ssem.at[offset], d_rsem.at[offset], across)

    def more_pair(offset, which):
        ref = quarter(offset, which, 0)
        return remote(ref, ref, p_ssem.at[2 * offset], p_rsem.at[2 * offset], pair)

    def start_a():
        for origin in range(2 * NX):
            remote(a_stage.at[origin], a_stage.at[origin], a_ssem.at[0], a_rsem.at[origin], sibling).wait_recv()
        for part in range(2):
            pieces = [a_stage[2 * origin + part].astype(F32) for origin in range(NX)]
            a_buf[z, :, part * PQ:(part + 1) * PQ] = jnp.concatenate(pieces, axis=0).astype(BF16)

    def start_t():
        @pl.when(mine)
        def _():
            for half in range(2):
                ref = quarter(0, l, half)
                remote(ref, ref, t_ssem.at[0], t_rsem.at[half], sibling).wait_recv()
                for way in range(2):
                    zt(way, half, 0, 0).start()
                to_pair(0, l, half).start()
                to_across(0, l, half).start()

    g_acc[...] = jnp.zeros_like(g_acc)

    def arrive_t(step):
        @pl.when(mine)
        def _():
            for half in range(2):
                for way in range(2):
                    if step <= last(way, half):
                        offset = got_offset(way, step)
                        zt(way, half, step, offset).wait_recv()
                        if step < last(way, half):
                            zt(way, half, step + 1, offset).start()
                        to_pair(offset, l, half).start()
                        to_across(offset, l, half).start()

    flying = []

    def arrived_a(half, step):
        for way in range(2):
            if step <= last(way, half):
                za(way, half, step, got_offset(way, step)).wait_recv()

    def pass_a(half, step):
        if step > 0:
            arrived_a(half, step - 1)
        if len(flying) >= WINDOW:
            for copy in flying.pop(0):
                copy.wait_send()
        copies = [za(way, half, step, sent_offset(way, step)) for way in range(2) if step <= last(way, half)]
        for copy in copies:
            copy.start()
        flying.append(copies)

    def relay(*offsets):
        @pl.when(mine)
        def _():
            for offset in offsets:
                to_pair(offset, 1 - l, 1).wait_recv()
                more_across(offset, 1 - l).start()

        @pl.when(other)
        def _():
            for offset in offsets:
                to_across(offset, 1 - l, 0).wait_recv()
                more_pair(offset, 1 - l).start()

    def complete(*offsets):
        @pl.when(mine)
        def _():
            for offset in offsets:
                to_pair(offset, 1 - l, 0).wait_recv()

        @pl.when(other)
        def _():
            for offset in offsets:
                to_across(offset, 1 - l, 1).wait_recv()
                more_across(offset, l).wait_recv()
                more_pair(offset, l).wait_recv()

    def b_arrived(s):
        ref = b_buf.at[s, b_rows(k)]
        remote(ref, ref, b_ssem.at[s], b_rsem.at[s], sibling).wait_recv()
        f_copy(s).start()

    def b_complete(s):
        if s == 0:
            b_stay(b_end).wait()
        ref = b_buf.at[s, b_rows(1 - k)]
        remote(ref, ref, f_ssem.at[s], f_rsem.at[s], sibling).wait_recv()

    groups = ((0, 1), (7, 2), (6, 3), (5,), (4,))

    places = [[2 * (sum(len(blocks) for blocks in groups[:g]) + i) + j for i in range(len(groups[g])) for j in range(2)]
              for g in range(len(groups))]

    def product(g, first, end):
        blocks = [block_of(offset) for offset in groups[g]]

        def one(b, carry):
            left = jnp.concatenate([a_buf[block] for block in blocks], axis=0)
            v = jnp.dot(left, b_buf[b], preferred_element_type=F32)
            high = v.astype(BF16)
            low = (v - high.astype(F32)).astype(BF16)
            for j, place in enumerate(places[g]):
                hl[place, rows(b * 160, 80)] = high[80 * j:80 * j + 80]
                hl[place, rows(b * 160 + 80, 80)] = low[80 * j:80 * j + 80]
            return carry

        lax.fori_loop(first, end, one, 0)

    def contract(g):
        for j, place in enumerate(places[g]):
            g_acc[...] += lax.dot_general(
                hl[place], t_buf[block_of(groups[g][j // 2]), 160 * (j % 2):160 * (j % 2) + 160],
                (((1,), (1,)), ((), ())), preferred_element_type=F32)

    start_t()
    start_a()
    start_b(3)
    pass_a(0, 0)
    arrive_t(0)
    pass_a(1, 0)
    relay(0)
    arrive_t(1)
    pass_a(0, 1)
    relay(7, 1)
    arrive_t(2)
    pass_a(1, 1)
    b_arrived(1)
    b_arrived(2)
    b_complete(0)
    product(0, 0, 1)
    b_complete(1)
    b_complete(2)
    product(0, 1, 3)
    relay(6, 2)
    b_arrived(3)
    pass_a(0, 2)
    arrive_t(3)
    pass_a(1, 2)
    b_complete(3)
    product(0, 3, 4)
    product(1, 0, 4)
    relay(5, 3)
    pass_a(0, 3)
    pass_a(1, 3)
    complete(0, 1)
    contract(0)
    complete(7, 2)
    contract(1)
    product(2, 0, 4)
    relay(4)
    complete(6, 3)
    contract(2)
    product(3, 0, 4)
    arrived_a(0, 3)
    arrived_a(1, 3)
    product(4, 0, 4)
    complete(5, 4)
    contract(3)
    contract(4)

    row = lax.broadcasted_iota(jnp.int32, (80, 160), 0)
    col = lax.broadcasted_iota(jnp.int32, (80, 160), 1)
    diagonal = (row // 4) == (col // 8)
    left = ((lax.broadcasted_iota(jnp.int32, (8, 80), 1) % 4) == lax.broadcasted_iota(jnp.int32, (8, 80), 0)).astype(F32)
    right = ((lax.broadcasted_iota(jnp.int32, (160, 128), 0) % 8)
             == lax.broadcasted_iota(jnp.int32, (160, 128), 1)).astype(F32)
    for s in range(NX):
        both = g_acc[160 * s:160 * s + 80] + g_acc[160 * s + 80:160 * s + 160]
        both = jnp.where(diagonal, both, 0.0)
        half = jnp.dot(left, both, precision=lax.Precision.HIGHEST, preferred_element_type=F32)
        r_send[s] = jnp.dot(half, right, precision=lax.Precision.HIGHEST, preferred_element_type=F32)

    q4 = l * 2 + k
    r_copies = []
    for s in (3, 1, 2, 0):
        for e in (2, 3, 1, 0):
            if s == 0 and e == 0:
                continue
            q = (q4 + e) % 4
            copy = remote(r_send.at[s], r_in.at[4 * s + e], r_ssem.at[4 * s + e], r_rsem.at[4 * s + e],
                          dev((x + NX - SLOTS[s]) % NX, z, h, q // 2, q % 2))
            copy.start()
            r_copies.append(copy)
    for i, copy in enumerate(a_copies):
        if i == 0:
            @pl.when(other)
            def _():
                copy.wait_send()
        else:
            copy.wait_send()
    for s in range(NX):
        f_copy(s, b_end).wait_send()
        if s:
            b_copy(s, b_end).wait_send()
    for copies in flying:
        for copy in copies:
            copy.wait_send()

    @pl.when(t_mine)
    def _():
        for copy in t_copies:
            copy.wait_send()

    @pl.when(mine)
    def _():
        for way in range(2):
            for half in range(2):
                for step in range(last(way, half) + 1):
                    zt(way, half, step, sent_offset(way, step)).wait_send()
        for offset in range(NZ):
            for part in range(2):
                to_pair(offset, l, part).wait_send()
                to_across(offset, l, part).wait_send()
            more_across(offset, 1 - l).wait_send()

    @pl.when(other)
    def _():
        for offset in range(NZ):
            more_pair(offset, 1 - l).wait_send()

    total = r_send[0]
    for copy in r_copies:
        copy.wait_recv()
    for i in range(1, 16):
        total = total + r_in[i]

    for load in energies:
        load.wait()
    row = lax.broadcasted_iota(jnp.int32, (4, 2), 0)
    col = lax.broadcasted_iota(jnp.int32, (4, 2), 1)
    lane = lax.broadcasted_iota(jnp.int32, (4, 128), 1)
    ladder = [jnp.sum(jnp.where(lane == 2 * q4 + i, total[:4], 0.0), axis=1, keepdims=True) for i in range(2)]
    ladder = jnp.where(col == 0, ladder[0], ladder[1])
    first = jnp.where(row == 0, va[0], jnp.where(row == 1, va[1], jnp.where(row == 2, va[2], va[3])))
    out[...] = ladder / (first + vb[0] - jnp.where(col == 0, occ[0], occ[1]))
    for copy in r_copies:
        copy.wait_send()


def body(chol_a, chol_b, amplitudes, vir_a, vir_b, occ_pair):
    b_in = chol_b.reshape(chol_b.shape[0], chol_b.shape[2])
    t_in = amplitudes.reshape(80, 640)
    dma = pltpu.SemaphoreType.DMA
    tile = pl.pallas_call(
        kernel,
        out_shape=jax.ShapeDtypeStruct((4, 2), F32),
        in_specs=[pl.BlockSpec(memory_space=pltpu.HBM)] * 6,
        out_specs=pl.BlockSpec(memory_space=pltpu.VMEM),
        scratch_shapes=[
            pltpu.SMEM((4,), F32),
            pltpu.SMEM((1,), F32),
            pltpu.SMEM((2,), F32),
            pltpu.VMEM(chol_a.shape, BF16),
            pltpu.VMEM(b_in.shape, BF16),
            pltpu.VMEM(t_in.shape, BF16),
            pltpu.VMEM((NX, 40, PQ), BF16),
            pltpu.VMEM((PQ, 640), BF16),
            pltpu.VMEM((2 * NX, 40, PQ), BF16),
            pltpu.VMEM((NZ, 160, 2 * PQ), BF16),
            pltpu.VMEM((NZ, 320, 640), BF16),
            pltpu.VMEM((NX, 2 * PQ, 640), BF16),
            pltpu.VMEM((16, 640, 640), BF16),
            pltpu.VMEM((640, 160), F32),
            pltpu.VMEM((NX, 8, 128), F32),
            pltpu.VMEM((16, 8, 128), F32),
            dma((8,)), dma((8,)), dma((4,)), dma((4,)), dma((4,)), dma((4,)), dma((4,)), dma((4,)),
            dma((16,)), dma((16,)), dma((16,)), dma((16,)), dma((16,)), dma((16,)), dma((16,)), dma((16,)), dma((8,)), dma((8,)),
            dma((16,)), dma((16,)), dma((7,)),
        ],
        compiler_params=pltpu.CompilerParams(
            collective_id=0, has_side_effects=True, vmem_limit_bytes=64 * 1000 * 1024),
        cost_estimate=pl.CostEstimate(flops=7_000_000_000, bytes_accessed=16_000_000, transcendentals=0),
    )(chol_a, b_in, t_in, vir_a, vir_b, occ_pair)
    return tile.reshape(4, 1, 2)


def solution(mesh):
    return jax.shard_map(
        body,
        mesh=mesh,
        in_specs=(
            P("vp", None, "ch"),
            P("ch", "vp", None),
            P("vp", None, None),
            P(),
            P("vp"),
            P("ch"),
        ),
        out_specs=P(None, "vp", "ch"),
        check_vma=False,
    )
```

time: 71 us -> 67.2 us (0.946)
  the two profiles are of different devices: /device:TPU:25 before, /device:TPU:1 now
where the time goes in v3:
time: 67.2 us; the launch traced here: 67 us
  Pallas kernels  65.1 us (97%)
  local copies, waits for them, and re-layouts  1.32 us (2%)
    pallas_call x1, Pallas kernels, body(): pl.pallas_call(kernel, out_shape=jax.ShapeDtypeStruct((4, 2), F32), in_sp...  65.1 us

profile of v3, /device:TPU:1, one launch (start us, length us, event | category | flops | bytes accessed | tf_op | source)
XLA Modules:
  0.0 67.0 jit_solution(16930692861095862880)
XLA Ops:
  0.7 65.1 %shard_map.64 = f32[4,2]{1,0:T(4,128)} custom-call(bf16[10,4,1500]{2,1,0:T(4,128)(2,1)} %a_hbm.1, bf16[1500,640]{1,0:T(8,128)(2,1)} %bitcast.3, bf16[80,640]{1,0:T(8,128)(2,1)} %bitcast.4, f32[4]{0:T(128)} %va_hbm.1, f32[1]{0:T(128)S(6)} %copy.8.vb_hbm, f32[2]{0:T(128)} %occ_hbm.1), custom_call_target="tpu_custom_call" | custom-call | flops 7000000000 | bytes 16000000 | tf_op jit(solution)/shard_map/pallas_call | solution.py:427
  65.7 1.3 %copy.7 = f32[4,2]{0,1:T(2,128)} copy(f32[4,2]{1,0:T(4,128)} %shard_map.64) | data formatting | bytes 64 | tf_op jit(solution)/shard_map/pallas_call | solution.py:427
